TPU v7x, 256 devices: a whole 4x4x8 slice. The times are simulated.
256 devices in a mesh: ctx: 32 (over z, x), head: 8 (over y, core).
Axes of the slice: x: 4, y: 4, z: 8, core: 2. Of those that a mesh axis runs over, the one named last changes fastest.
Arguments:
- query_states: bfloat16 [16384, 4096], P('ctx', 'head'), may hold values from -12 to 12
- key_states: bfloat16 [16384, 4096], P('ctx', 'head'), may hold values from -12 to 12
- value_states: bfloat16 [16384, 4096], P('ctx', 'head'), may hold values from -6 to 6
- out_weight: bfloat16 [4096, 4096], P('head'), may hold values from -0.5 to 0.5
- doc_reset: int32 [128], P('ctx'), may hold values from 0 to 255
- rand_group: int32 [128, 3], P('ctx'), may hold values from 0 to 31, all different within a row; in each aligned block of 4 rows (0 to 3, 4 to 7, ...) at most 2 rows name the same one
- rand_slot: int32 [128, 3], P('ctx'), may hold values from 0 to 3
- global_blocks: int32 [2], replicated, may hold values from 0 to 127, as said below
Outputs:
- layer_out: bfloat16 [16384, 4096], P(('ctx', 'head'))
Inputs may be any that keep to these rules, and one draw needn't show every extreme that they name: `doc_reset`: A value of 128 or more means that no document starts in the block. `rand_group`: the 3 groups of one row differ. In the rows of one device's 4 query blocks no group is named more than 2 times, and in some device's rows some group is named exactly 2 times. `global_blocks`: the 2 global blocks differ, and one of them is the sequence's last block.
All inputs are finite; a program needn't handle non-finite values.
Results may differ from a plain program's by a relative error of at most 0.019.
The roundings to bfloat16 on the way count: a program that leaves them out, or rounds other values in their place, can miss the bound.
Values may be sent and summed in bfloat16 or wider, within the bound.
A program may use at most 128 MiB of HBM per device.

v0:
```python
import math

import jax
import jax.numpy as jnp
from jax import lax
from jax.sharding import PartitionSpec as P

HD = 128


ROPE_BASE = 500000.0


def carried_in(part, axis, combine, identity):
    place = lax.axis_index(axis)
    gathered = lax.all_gather(part, axis)
    state = jnp.zeros_like(part) + jnp.asarray(identity, part.dtype)

    def one(hop, state):
        return combine(state, lax.dynamic_index_in_dim(gathered, hop, 0, False))

    return lax.fori_loop(0, place, one, state)


def padded(block, sides, width):
    for axis, dim in sides:
        count = lax.axis_size(axis)
        forward = [(i, i + 1) for i in range(count - 1)]
        backward = [(target, source) for source, target in forward]
        low = lax.ppermute(
            lax.slice_in_dim(block, block.shape[dim] - width, None, axis=dim), axis, forward
        )
        high = lax.ppermute(lax.slice_in_dim(block, 0, width, axis=dim), axis, backward)
        block = jnp.concatenate([low, block, high], axis=dim)
    return block


def spread(value, axis, source):
    kept = jnp.where(lax.axis_index(axis) == source, value, 0).astype(value.dtype)
    return lax.psum(kept, axis)


def rope_tables(position, head_dim):
    half_dim = head_dim // 2
    exponent = jnp.arange(half_dim, dtype=jnp.float32) * (2.0 / head_dim)
    inv_freq = jnp.exp(-exponent * math.log(ROPE_BASE))
    angles = position.astype(jnp.float32)[:, None] * inv_freq[None, :]
    return (jnp.cos(angles), jnp.sin(angles))


def rotate(states, position, head_dim):
    row_total = states.shape[0]
    half_dim = head_dim // 2
    shaped = states.astype(jnp.float32).reshape(row_total, -1, head_dim)
    cosine, sine_table = rope_tables(position, head_dim)
    cosine = cosine[:, None, :]
    sine_table = sine_table[:, None, :]
    first_half = shaped[..., :half_dim]
    second_half = shaped[..., half_dim:]
    turned = jnp.concatenate(
        [
            first_half * cosine - second_half * sine_table,
            second_half * cosine + first_half * sine_table,
        ],
        axis=-1,
    )
    return turned.reshape(row_total, -1).astype(jnp.bfloat16)


def part_attention(query_part, key_part, value_part, key_valid, head_dim):
    scores = jnp.einsum(
        "...qhd,...khd->...hqk", query_part, key_part, preferred_element_type=jnp.float32
    ) * head_dim ** (-0.5)
    if key_valid is not None:
        scores = jnp.where(key_valid, scores, -jnp.inf)
    row_max = jnp.max(scores, axis=-1)
    weights = jnp.exp(scores - row_max[..., None]).astype(jnp.bfloat16)
    row_total = jnp.sum(weights, axis=-1, dtype=jnp.float32)
    partial_value = jnp.einsum(
        "...hqk,...khd->...qhd", weights, value_part, preferred_element_type=jnp.float32
    ).astype(jnp.bfloat16)
    return (row_max, row_total, partial_value)


def merge_parts(tops, totals, partials):
    highest = jnp.max(tops, axis=-3, keepdims=True)
    factor = jnp.exp(tops - highest)
    denominator = jnp.sum(factor * totals, axis=-3)
    factor_rows = jnp.swapaxes(factor, -1, -2)[..., None]
    numerator = jnp.sum(factor_rows * partials.astype(jnp.float32), axis=-4)
    merged = numerator / jnp.swapaxes(denominator, -1, -2)[..., None]
    return merged.astype(jnp.bfloat16)


def request_rank(flat_groups):
    item_count = flat_groups.shape[-1]
    order_ids = jnp.arange(item_count)
    same_group = (flat_groups[..., :, None] == flat_groups[..., None, :]) & (
        order_ids[:, None] > order_ids[None, :]
    )
    return jnp.sum(same_group, axis=-1)


def on_device(
    query_states,
    key_states,
    value_states,
    out_weight,
    doc_reset,
    rand_group,
    rand_slot,
    global_blocks,
):
    block_count = doc_reset.shape[0]
    token_count = query_states.shape[0]
    block_len = token_count // block_count
    head_dim = HD
    feature_width = query_states.shape[1]
    local_heads = feature_width // head_dim
    rand_count = rand_group.shape[1]
    groups = lax.axis_size("ctx")
    my_group = lax.axis_index("ctx")
    total_blocks = groups * block_count
    capacity = max(2, -(-(block_count * rand_count) // groups))
    first_block = my_group * block_count
    block_ids = first_block + jnp.arange(block_count, dtype=jnp.int32)
    reset_pos = jnp.where(doc_reset < block_len, block_ids * block_len + doc_reset, 0)
    local_last = jnp.max(reset_pos)
    carried = carried_in(local_last, "ctx", jnp.maximum, jnp.int32(0))
    running = jnp.maximum(lax.cummax(reset_pos), carried)
    previous = jnp.concatenate([carried[None], running[:-1]])
    offsets = jnp.arange(block_len, dtype=jnp.int32)
    token_start = jnp.where(
        offsets[None, :] >= doc_reset[:, None], reset_pos[:, None], previous[:, None]
    )
    tokens = block_ids[:, None] * block_len + offsets[None, :]
    position = (tokens - token_start).reshape(-1)
    rot_q = rotate(query_states, position, head_dim)
    rot_k = rotate(key_states, position, head_dim)
    paired = jnp.concatenate([rot_k, value_states], axis=1)
    own_blocks = paired.reshape(block_count, block_len, 2 * feature_width)
    query_tiles = rot_q.reshape(block_count, block_len, local_heads, head_dim)
    extended = padded(paired, (("ctx", 0),), block_len)
    edge_blocks = extended.reshape(block_count + 2, block_len, 2 * feature_width)
    window = jnp.concatenate([edge_blocks[:-2], edge_blocks[1:-1], edge_blocks[2:]], axis=1)
    fetched = []
    for glob_num in range(global_blocks.shape[0]):
        target = global_blocks[glob_num]
        owner_dev = target // block_count
        block_piece = lax.dynamic_index_in_dim(own_blocks, target % block_count, 0, keepdims=False)
        fetched.append(spread(block_piece, "ctx", owner_dev))
    global_rows = jnp.concatenate(fetched, axis=0)
    glob_total = global_rows.shape[0]
    local_keys = jnp.concatenate(
        [window, jnp.broadcast_to(global_rows[None], (block_count, glob_total, 2 * feature_width))],
        axis=1,
    )
    local_keys = local_keys.reshape(
        block_count, 3 * block_len + glob_total, 2, local_heads, head_dim
    )
    always = jnp.ones((block_count, 1), bool)
    block_flags = jnp.concatenate(
        [
            (block_ids > 0)[:, None],
            always,
            (block_ids < total_blocks - 1)[:, None],
            jnp.ones((block_count, global_blocks.shape[0]), bool),
        ],
        axis=1,
    )
    key_valid = jnp.repeat(block_flags, block_len, axis=1)[:, None, None, :]
    local_part = part_attention(
        query_tiles, local_keys[:, :, 0], local_keys[:, :, 1], key_valid, head_dim
    )
    table_group, table_slot = (
        lax.all_gather(rand_group, "ctx", axis=0, tiled=True),
        lax.all_gather(rand_slot, "ctx", axis=0, tiled=True),
    )
    table_flat = table_group.reshape(groups, -1)
    slot_flat = table_slot.reshape(groups, -1)
    table_rank = request_rank(table_flat)
    slot_ids = jnp.arange(capacity)
    slot_hit = (table_flat == my_group)[..., None] & (table_rank[..., None] == slot_ids)
    send_slot = jnp.sum(jnp.where(slot_hit, slot_flat[..., None], 0), axis=1)
    own_flat = rand_group.reshape(-1)
    own_rank = request_rank(own_flat)
    source_index = own_flat * capacity + own_rank
    outgoing = own_blocks[send_slot]
    incoming = lax.all_to_all(outgoing, "ctx", split_axis=0, concat_axis=0, tiled=True)
    chosen = incoming.reshape(groups * capacity, block_len, 2 * feature_width)[source_index]
    chosen = chosen.reshape(block_count, rand_count, block_len, 2, local_heads, head_dim)
    query_many = jnp.broadcast_to(
        query_tiles[:, None], (block_count, rand_count, block_len, local_heads, head_dim)
    )
    random_top, random_total, random_partial = part_attention(
        query_many, chosen[:, :, :, 0], chosen[:, :, :, 1], None, head_dim
    )
    tops = jnp.concatenate([local_part[0][:, None], random_top], axis=1)
    totals = jnp.concatenate([local_part[1][:, None], random_total], axis=1)
    partials = jnp.concatenate([local_part[2][:, None], random_partial], axis=1)
    attention = merge_parts(tops, totals, partials).reshape(token_count, feature_width)
    return lax.psum_scatter(
        jnp.dot(attention, out_weight, preferred_element_type=jnp.float32).astype(jnp.bfloat16),
        "head",
        scatter_dimension=0,
        tiled=True,
    )


def solution(mesh):
    placed = (
        P("ctx", "head"),
        P("ctx", "head"),
        P("ctx", "head"),
        P("head", None),
        P("ctx"),
        P("ctx", None),
        P("ctx", None),
        P(),
    )
    return jax.shard_map(
        on_device, mesh=mesh, in_specs=placed, out_specs=P(("ctx", "head"), None), check_vma=False
    )
```

profile of v0, /device:TPU:1, one launch (start us, length us, event | category | flops | bytes accessed | tf_op | source)
XLA Modules:
  0.0 610.0 jit_solution(5231638643541279438)
XLA Ops:
  6.5 1.4 dynamic-slice
  7.9 1.3 fusion.23
  9.3 1.4 dynamic-update-slice
  10.6 19.8 %all-reduce = s32[32]{0:T(128)S(1)} all-reduce(s32[32]{0:T(128)S(1)} %dynamic-update-slice), channel_id=1, replica_groups=mesh['ctx'=32,'head'=8] {'ctx'}, use_global_device_ids=true, to_apply=%add | all-reduce | flops 32 | bytes 256
  34.8 3.5 collective-permute-start
  39.7 70.9 %all-gather.1 = s32[32,4,3]{2,1,0:T(4,128)S(1)} all-gather(s32[1,4,3]{2,1,0:T(4,128)S(1)} %bitcast.120), channel_id=1, replica_groups=mesh['ctx'=32,'head'=8] {'ctx'}, dimensions={0}, use_global_device_ids=true | all-gather | bytes 1584 | tf_op jit(solution)/shard_map/all_gather | solution.py:177
  110.7 35.2 %all-gather = s32[32,4,3]{2,1,0:T(4,128)S(1)} all-gather(s32[1,4,3]{2,1,0:T(4,128)S(1)} %bitcast.119), channel_id=1, replica_groups=mesh['ctx'=32,'head'=8] {'ctx'}, dimensions={0}, use_global_device_ids=true | all-gather | bytes 1584 | tf_op jit(solution)/shard_map/all_gather | solution.py:176
  146.4 1.6 pad_maximum_fusion.4
  148.6 7.3 %gather_fusion = bf16[64,128,1024]{2,1,0:T(8,128)(2,1)} fusion(bf16[4,128,1024]{2,1,0:T(8,128)(2,1)S(1)} %bitcast.100, s32[1024]{0:T(1024)S(1)} %pad_clamp_fusion.1), kind=kCustom, calls=%fused_computation | custom fusion | bytes 33554688 | tf_op jit(solution)/shard_map/gather | solution.py:188
  155.9 5.3 all-to-all-start
  170.3 1.3 reshape.322
  172.4 2.2 reshape.324
  174.6 1.7 copy.160
  176.3 2.4 copy.159
  178.7 324.9 %all-reduce.4.cloned.1.call-done = (bf16[128,1024]{1,0:T(8,128)(2,1)}, bf16[128,1024]{1,0:T(8,128)(2,1)}) async-done(((bf16[128,1024]{1,0:T(8,128)(2,1)}, bf16[128,1024]{1,0:T(8,128)(2,1)}), (bf16[128,1024]{1,0:T(8,128)(2,1)}, bf16[128,1024]{1,0:T(8,128)(2,1)})) %all-reduce.4.cloned.1.call-update) | async-done | bytes 524304 | tf_op jit(solution)/shard_map/psum | solution.py:40
  505.7 1.3 copy.157
  508.3 4.7 pad_maximum_fusion
  514.1 1.4 convert_reduce_fusion
  515.5 2.8 fusion.6
  518.3 6.5 %gather_fusion.1 = bf16[12,128,1024]{2,1,0:T(8,128)(2,1)S(1)} fusion(bf16[64,128,1024]{2,1,0:T(8,128)(2,1)} %bitcast.25, s32[1024]{0:T(1024)S(1)} %pad_clamp_fusion), kind=kCustom, calls=%fused_computation.1 | custom fusion | bytes 6291504 | tf_op jit(solution)/shard_map/gather | solution.py:190
  524.8 2.8 copy.166
  527.6 3.0 multiply_reduce_fusion.2
  533.6 6.5 %convolution_convert_fusion = bf16[512,4096]{1,0:T(8,128)(2,1)} fusion(bf16[512,4096]{1,0:T(8,128)(2,1)} %param.13, bf16[64,8,4,128]{3,2,1,0:T(4,128)(2,1)S(1)} %bitcast.112), kind=kOutput, calls=%fused_computation.2 | convolution fusion | flops 2149580800 | bytes 8912896 | tf_op jit(solution)/shard_map/dot_general | solution.py:203
  540.1 63.1 %reduce-scatter.2.cloned.1.call-done = bf16[64,4096]{1,0:T(8,128)(2,1)} async-done(((bf16[512,4096]{1,0:T(8,128)(2,1)}), bf16[64,4096]{1,0:T(8,128)(2,1)}) %reduce-scatter.2.cloned.1.call-update) | async-done | bytes 524304 | tf_op jit(solution)/shard_map/reduce_scatter | solution.py:202
  (86 shorter events, 18.9 us)
Async XLA Ops:
  6.5 26.8 %copy-start.4 = (bf16[512,512]{1,0:T(8,128)(2,1)S(1)}, bf16[512,512]{1,0:T(8,128)(2,1)}, u32[]{:S(2)}) copy-start(bf16[512,512]{1,0:T(8,128)(2,1)} %param.11) | copy-start | bytes 1572868
  30.7 3.1 copy-start.8
  33.8 5.8 copy-start.6
  34.4 76.3 %copy-start.5 = (s32[4,3]{1,0:T(4,128)S(1)}, s32[4,3]{1,0:T(4,128)}, u32[]{:S(2)}) copy-start(s32[4,3]{1,0:T(4,128)} %param.15) | copy-start | bytes 148
  34.8 111.6 %collective-permute-start = (bf16[128,1024]{0,1:T(8,128)(2,1)S(1)}, bf16[128,1024]{0,1:T(8,128)(2,1)S(1)}, u32[]{:S(2)}, u32[]{:S(2)}) collective-permute-start(bf16[128,1024]{0,1:T(8,128)(2,1)S(1)} %get-tuple-element.50), channel_id=1, source_target_pairs={{0,8},{8,16},{16,24},{24,32},{32,40},{40,48},{48,56},{56,64},{64,7... | collective-permute-start | bytes 786440 | tf_op jit(solution)/shard_map/ppermute | solution.py:30
  38.3 108.1 %collective-permute-start.1 = (bf16[128,1024]{0,1:T(8,128)(2,1)S(1)}, bf16[128,1024]{0,1:T(8,128)(2,1)S(1)}, u32[]{:S(2)}, u32[]{:S(2)}) collective-permute-start(bf16[128,1024]{0,1:T(8,128)(2,1)S(1)} %get-tuple-element.51), channel_id=1, source_target_pairs={{8,0},{16,8},{24,16},{32,24},{40,32},{48,40},{56,48},{64,56},{72,6... | collective-permute-start | bytes 786440 | tf_op jit(solution)/shard_map/ppermute | solution.py:33
  155.9 5.4 copy-start.7
  155.9 362.4 %all-to-all-start = ((bf16[32,2,128,1024]{3,2,1,0:T(8,128)(2,1)}), bf16[32,2,128,1024]{3,2,1,0:T(8,128)(2,1)}, u32[]{:S(2)}, u32[]{:S(2)}) async-start(bf16[32,2,128,1024]{3,2,1,0:T(8,128)(2,1)} %bitcast.102), calls=%async_computation | async-start | bytes 33554432 | tf_op jit(solution)/shard_map/all_to_all | solution.py:189
  161.2 342.5 %all-reduce.4.cloned.1.call-start = ((), (), s32[]{:S(2)}) async-start(), calls=%async_computation.3 | async-start | bytes 1048576 | tf_op jit(solution)/shard_map/psum | solution.py:40
  168.4 434.8 %reduce-scatter.2.cloned.1.call-start = ((), (), s32[]{:S(2)}) async-start(), calls=%async_computation.2 | async-start | bytes 4718592 | tf_op jit(solution)/shard_map/reduce_scatter | solution.py:202
  168.9 344.0 %copy-start.1 = (bf16[512,4,128]{2,0,1:T(8,128)(2,1)}, bf16[512,4,128]{2,0,1:T(8,128)(2,1)S(1)}, u32[]{:S(2)}) copy-start(bf16[512,4,128]{2,0,1:T(8,128)(2,1)S(1)} %copy.149) | copy-start | bytes 1572868
  507.1 1.2 copy-start.2
  527.6 3.0 copy-start
  531.3 1.3 copy-start.3
Sparse Core Ops, SparseCore 0:
  168.5 335.1 all-reduce.3
  540.2 62.9 reduce-scatter.1
where the time goes:
time: 613 us; the launch traced here: 610 us
  waiting for transfers between devices  388 us (63%)
  blocking collectives  126 us (21%)
  local copies, waits for them, and re-layouts  37.8 us (6%)
  between operations  18.9 us (3%)
  other arithmetic  14.9 us (2%)
  matrix products  14 us (2%)
  starting transfers between devices  10.4 us (2%)
    psum x1, waiting for transfers between devices, spread(): return lax.psum(kept, axis)  325 us
    all_gather x1, blocking collectives, on_device(): lax.all_gather(rand_slot, 'ctx', axis=0, tiled=True)  70.9 us
    reduce_scatter x1, waiting for transfers between devices, on_device(): lax.psum_scatter(jnp.dot(attention, out_weight, preferred_element_type=jn...  63.1 us
    all_gather x1, blocking collectives, on_device(): lax.all_gather(rand_group, 'ctx', axis=0, tiled=True)  35.2 us
    unnamed x1, blocking collectives  19.8 us
  transfers between devices with their start and end apart: 5, of which 2 were waited for; matrix products, arithmetic and copies ran while one was open for 4% of the time, Pallas kernels for 0%

commit v1 on v0

v1 whole, which is shorter than its diff:
```python
import math

import jax
import jax.numpy as jnp
import numpy as np
from jax import lax
from jax.experimental import pallas as pl
from jax.experimental.pallas import tpu as pltpu
from jax.sharding import PartitionSpec as P

HD = 128
BLK = 128
NZ, NX, NY = 8, 4, 4
GT = 512
WIDTH = 4096
TILE = 512
ROPE_BASE = 500000.0
MESH = pl.DeviceIdType.MESH
F32 = jnp.float32
BF16 = jnp.bfloat16
SCORE_SCALE = HD ** (-0.5) * math.log2(math.e)


def sin_cos(angle):
    turns = jnp.floor(angle * (2.0 / math.pi) + 0.5)
    r = angle - turns * 1.5703125
    r = r - turns * 4.837512969970703125e-4
    r = r - turns * 7.54978995489188216e-8
    quarter = turns - 4.0 * jnp.floor(turns * 0.25)
    z = r * r
    s = r + r * z * (-1.6666654611e-1 + z * (8.3321608736e-3 + z * -1.9515295891e-4))
    c = 1.0 - 0.5 * z + z * z * (
        4.166664568298827e-2 + z * (-1.388731625493765e-3 + z * 2.443315711809948e-5)
    )
    odd = (quarter == 1.0) | (quarter == 3.0)
    sine = jnp.where(odd, c, s)
    cosine = jnp.where(odd, s, c)
    sine = jnp.where(quarter >= 2.0, -sine, sine)
    cosine = jnp.where((quarter == 1.0) | (quarter == 2.0), -cosine, cosine)
    return sine, cosine


def kernel(
    q_hbm, k_hbm, v_hbm, w_hbm, meta_ref, freq_ref, glob_ref, out_ref,
    qin, kin, qrot, krot, qbuf, kbuf, vbuf, wbuf, mall, meta_s, cos_t, sin_t,
    osend, obuf, st1, st2, st3, sa, sb, ra, rb, total,
    in_sem, w_sem, w_send, w_recv,
    mz_send, mz_recv, mx_send, mx_recv, ms_sem,
    z_send, z_recv, x_send, f_send, l_recv, r_recv, f_recv, s_send, s_recv,
    o_send, o_recv, y_send, y_recv,
):
    ctx = lax.axis_index("ctx")
    head = lax.axis_index("head")
    z, x = ctx // NX, ctx % NX
    y, c = head // 2, head % 2
    xr, xl = (x + 1) % NX, (x + NX - 1) % NX
    yr, yl = (y + 1) % NY, (y + NY - 1) % NY
    yo = (y + 2) % NY
    xo = (x + 2) % NX

    def dev(zz, xx, yy, cc):
        return (zz * NX + xx, yy * 2 + cc)

    sib = dev(z, x, y, 1 - c)

    def local(src, dst, sem):
        return pltpu.make_async_copy(src, dst, sem)

    def remote(src, dst, ssem, rsem, to):
        return pltpu.make_async_remote_copy(
            src_ref=src, dst_ref=dst, send_sem=ssem, recv_sem=rsem, device_id=to, device_id_type=MESH
        )

    def arrived(dst, sem):
        pltpu.make_async_copy(dst, dst, sem).wait()

    copy_k = local(k_hbm, kin, in_sem.at[0])
    copy_q = local(q_hbm, qin, in_sem.at[1])
    copy_k.start()
    copy_q.start()

    barrier = pltpu.get_barrier_semaphore()
    for d in range(NZ):
        for e in range(2):
            if d or e:
                pl.semaphore_signal(
                    barrier, inc=1, device_id=dev((z + d) % NZ, x, y, (c + e) % 2), device_id_type=MESH
                )
    for xx in (xr, xl, xo):
        pl.semaphore_signal(barrier, inc=1, device_id=dev(z, xx, y, c), device_id_type=MESH)
    for yy in (yr, yl):
        pl.semaphore_signal(barrier, inc=1, device_id=dev(z, x, yy, c), device_id_type=MESH)
    pl.semaphore_wait(barrier, 2 * NZ - 1 + 3 + 2)

    meta_z = []
    for d in range(1, NZ):
        cp = remote(meta_ref, mall.at[x, z], mz_send.at[d - 1], mz_recv.at[d - 1], dev((z + d) % NZ, x, y, c))
        cp.start()
        meta_z.append(cp)
    mall[x, z] = meta_ref[...]

    def rows_of(group):
        return pl.ds(group * 4, 4)

    own_rows = rows_of(ctx)
    target_core = z % 2

    def z_start(t, j, src, dst):
        row = 4 * c + j
        same = (row == z) & (target_core == c)
        send, recv = z_send.at[t, j], z_recv.at[t, z // 2]

        @pl.when(same)
        def _():
            local(src, dst, recv).start()

        @pl.when(jnp.logical_not(same))
        def _():
            remote(src, dst, send, recv, dev(row, x, y, target_core)).start()

    def z_done(t, j, src, dst):
        row = 4 * c + j
        same = (row == z) & (target_core == c)

        @pl.when(jnp.logical_not(same))
        def _():
            remote(src, dst, z_send.at[t, j], z_recv.at[t, z // 2], dev(row, x, y, target_core)).wait_send()

    q_rows = pl.ds((z // 2) * 4, 4)

    def v_src(j):
        return v_hbm.at[:, :, j * HD : (j + 1) * HD]

    for j in range(4):
        z_start(0, j, v_src(j), vbuf.at[own_rows])

    w_rows = pl.ds(pl.multiple_of(c * GT, GT), GT)
    w_other = pl.ds(pl.multiple_of((1 - c) * GT, GT), GT)
    copy_w = remote(w_hbm, wbuf.at[w_rows], w_send, w_recv, sib)
    copy_w.start()
    keep_w = local(w_hbm, wbuf.at[w_rows], w_sem)
    keep_w.start()

    for cp in meta_z:
        cp.wait_recv()
    meta_x = []
    for d in range(1, NX):
        cp = remote(mall.at[x], mall.at[x], mx_send.at[d - 1], mx_recv.at[d - 1], dev(z, (x + d) % NX, y, c))
        cp.start()
        meta_x.append(cp)
    copy_s = local(mall.at[x], meta_s, ms_sem)
    copy_s.start()
    for cp in meta_x:
        cp.wait_recv()

    doc = mall[:, :, 0, :].astype(F32)
    group_ids = lax.broadcasted_iota(jnp.int32, (NX, NZ, HD), 1) * NX + lax.broadcasted_iota(
        jnp.int32, (NX, NZ, HD), 0
    )
    lane = lax.broadcasted_iota(jnp.int32, (NX, NZ, HD), 2)
    block_ids = group_ids * 4 + lane
    starts = jnp.where((lane < 4) & (doc < float(BLK)), block_ids.astype(F32) * float(BLK) + doc, 0.0)
    own_doc = meta_ref[0:1, :].astype(F32)
    offset = lax.broadcasted_iota(jnp.int32, (BLK, HD), 0).astype(F32)
    half_sign = jnp.where(lax.broadcasted_iota(jnp.int32, (BLK, HD), 1) < HD // 2, -1.0, 1.0)
    for b in range(4):
        block = ctx * 4 + b
        before = jnp.where(block_ids < block, starts, 0.0)
        before = jnp.max(jnp.max(before, axis=0), axis=0, keepdims=True)
        before = jnp.max(before, axis=1, keepdims=True)
        reset = own_doc[0:1, b : b + 1]
        first = (block * BLK).astype(F32)
        begin = jnp.where(offset >= reset, first + reset, before)
        angle = (first + offset - begin) * freq_ref[0:1, :]
        sine, cosine = sin_cos(angle)
        cos_t[b * BLK : (b + 1) * BLK, :] = cosine
        sin_t[b * BLK : (b + 1) * BLK, :] = sine * half_sign

    def rotate(src, dst, j):
        @pl.loop(0, 4)
        def _(b):
            rows = pl.ds(pl.multiple_of(b * BLK, BLK), BLK)
            value = src[rows, j * HD : (j + 1) * HD].astype(F32)
            turned = value * cos_t[rows, :] + pltpu.roll(value, HD // 2, 1) * sin_t[rows, :]
            dst[j, b] = turned.astype(BF16)

    copy_k.wait()
    for j in range(4):
        rotate(kin, krot, j)
        z_start(1, j, krot.at[j], kbuf.at[own_rows])

    bufs = (vbuf, kbuf)

    def group_from(i, xx):
        return (2 * i + c) * NX + xx

    def x_out(t, i, k, to_x, recv):
        piece = bufs[t].at[rows_of(group_from(i, x))]
        return remote(piece, piece, x_send.at[t, i, k], recv.at[t, i], dev(z, to_x, y, c))

    def share(t, k, i, xx):
        piece = bufs[t].at[rows_of(group_from(i, xx))]
        return remote(piece, piece, s_send.at[t, k, i], s_recv.at[t, k, i], sib)

    def forward(t, i):
        from_x = jnp.where(c == 0, xl, xr)
        to_x = jnp.where(c == 0, xr, xl)
        piece = bufs[t].at[rows_of(group_from(i, from_x))]
        return remote(piece, piece, f_send.at[t, i], f_recv.at[t, i], dev(z, to_x, y, c))

    def own_step(t):
        @pl.loop(0, 4)
        def _(i):
            arrived(bufs[t].at[rows_of(group_from(i, x))], z_recv.at[t, i])
            x_out(t, i, 0, xr, l_recv).start()
            x_out(t, i, 1, xl, r_recv).start()
            share(t, 0, i, x).start()

    def side_step(t):
        @pl.loop(0, 4)
        def _(i):
            arrived(bufs[t].at[rows_of(group_from(i, xl))], l_recv.at[t, i])

            @pl.when(c == 0)
            def _():
                forward(t, i).start()

            share(t, 1, i, xl).start()
            arrived(bufs[t].at[rows_of(group_from(i, xr))], r_recv.at[t, i])

            @pl.when(c == 1)
            def _():
                forward(t, i).start()

            share(t, 2, i, xr).start()

    def far_step(t):
        @pl.loop(0, 4)
        def _(i):
            arrived(bufs[t].at[rows_of(group_from(i, xo))], f_recv.at[t, i])
            share(t, 3, i, xo).start()

    own_step(0)
    copy_q.wait()
    for j in range(4):
        rotate(qin, qrot, j)
        z_start(2, j, qrot.at[j], qbuf.at[q_rows])
    side_step(0)
    own_step(1)
    far_step(0)
    side_step(1)
    far_step(1)

    def from_sibling(t):
        @pl.loop(0, 4)
        def _(i):
            group = (2 * i + 1 - c) * NX
            for k, xx in enumerate((x, xl, xr, xo)):
                arrived(bufs[t].at[rows_of(group + xx)], s_recv.at[t, k, i])

    from_sibling(0)
    from_sibling(1)

    @pl.loop(0, 4)
    def _(i):
        arrived(qbuf.at[pl.ds(i * 4, 4)], z_recv.at[2, i])

    copy_s.wait()

    ones = jnp.ones((8 * BLK, HD), BF16)
    order = (yo, yr, yl, y)

    def o_copies(step, b, i):
        zz = 2 * i + c
        for e in range(2):
            src = osend.at[step, i, pl.ds(e * 64, 64)]
            dst = obuf.at[b * NZ + z]
            yield e, (zz == z) & (c == e), src, dst, dev(zz, x, y, e)

    def attend(step):
        b = order[step]

        @pl.loop(0, 4)
        def _(i):
            zz = 2 * i + c
            block = (zz * NX + x) * 4 + b
            ids = [
                jnp.maximum(block - 1, 0),
                block,
                jnp.minimum(block + 1, 127),
                glob_ref[0],
                glob_ref[1],
                meta_s[zz, 0, 4 + b * 3],
                meta_s[zz, 0, 5 + b * 3],
                meta_s[zz, 0, 6 + b * 3],
            ]
            q = qbuf[i * 4 + b]
            keys = jnp.concatenate([kbuf[n] for n in ids], axis=0)
            scores = lax.dot_general(q, keys, (((1,), (1,)), ((), ())), preferred_element_type=F32)
            low = jnp.where(block > 0, 0.0, -1e30).astype(F32)
            high = jnp.where(block < 127, 0.0, -1e30).astype(F32)
            scores = jnp.concatenate(
                [
                    scores[:, :BLK] + low,
                    scores[:, BLK : 2 * BLK],
                    scores[:, 2 * BLK : 3 * BLK] + high,
                    scores[:, 3 * BLK :],
                ],
                axis=1,
            ) * SCORE_SCALE
            top = jnp.max(scores, axis=1, keepdims=True)
            weights = jnp.exp2(scores - top).astype(BF16)
            values = jnp.concatenate([vbuf[n] for n in ids], axis=0)
            both = jnp.dot(weights, jnp.concatenate([values, ones], axis=1), preferred_element_type=F32)
            osend[step, i] = (both[:, :HD] / both[:, HD:]).astype(BF16)
            for e, same, src, dst, to in o_copies(step, b, i):

                @pl.when(same)
                def _():
                    local(src, dst, o_recv.at[step]).start()

                @pl.when(jnp.logical_not(same))
                def _():
                    remote(src, dst, o_send.at[step, i, e], o_recv.at[step], to).start()

    def outputs_of(step):
        b = order[step]
        arrived(obuf.at[pl.ds(b * NZ, NZ)], o_recv.at[step])
        return b

    def project(b, first, last, finish):
        @pl.loop(first, last)
        def _(n):
            cols = pl.ds(pl.multiple_of(n * TILE, TILE), TILE)
            rows = jnp.concatenate([obuf[b * NZ + m] for m in range(NZ)], axis=1)
            finish(cols, jnp.dot(rows, wbuf[:, cols], preferred_element_type=F32))

    half = WIDTH // 2
    tiles = WIDTH // TILE
    left, right = pl.ds(0, half), pl.ds(half, half)

    def y_copy(k, src, dst, yy):
        return remote(src, dst, y_send.at[k], y_recv.at[k], dev(z, x, yy, c))

    y_copies = [
        y_copy(0, st1.at[:, left], sa, yr),
        y_copy(1, st1.at[:, right], sb, yl),
        y_copy(2, st2.at[:, right], ra.at[:, right], yr),
        y_copy(3, st2.at[:, left], ra.at[:, left], yr),
        y_copy(4, st3.at[:, left], rb.at[:, left], yl),
        y_copy(5, st3.at[:, right], rb.at[:, right], yl),
    ]

    def put(ref):
        def finish(cols, tile):
            ref[:, cols] = tile.astype(ref.dtype)

        return finish

    def project_0():
        b = outputs_of(0)
        project(b, 0, tiles // 2, put(st1))
        y_copies[0].start()
        project(b, tiles // 2, tiles, put(st1))
        y_copies[1].start()

    def project_1():
        b = outputs_of(1)
        project(b, tiles // 2, tiles, put(st2))
        y_copies[2].start()
        y_copies[0].wait_recv()

        def finish(cols, tile):
            st2[:, cols] = (tile + sa[:, cols].astype(F32)).astype(BF16)

        project(b, 0, tiles // 2, finish)
        y_copies[3].start()

    def project_2():
        b = outputs_of(2)
        project(b, 0, tiles // 2, put(st3))
        y_copies[4].start()
        y_copies[1].wait_recv()

        @pl.loop(tiles // 2, tiles)
        def _(n):
            cols = pl.ds(pl.multiple_of(n * TILE, TILE), TILE)
            near = pl.ds(pl.multiple_of(n * TILE - half, TILE), TILE)
            rows = jnp.concatenate([obuf[b * NZ + m] for m in range(NZ)], axis=1)
            tile = jnp.dot(rows, wbuf[:, cols], preferred_element_type=F32)
            st3[:, cols] = (tile + sb[:, near].astype(F32)).astype(BF16)

        y_copies[5].start()

    def project_3():
        b = outputs_of(3)
        project(b, 0, tiles, put(total))

    attend(0)
    attend(1)
    keep_w.wait()
    copy_w.wait_send()
    arrived(wbuf.at[w_other], w_recv)
    project_0()
    attend(2)
    project_1()
    attend(3)
    project_2()
    project_3()
    for k in (2, 3, 4, 5):
        y_copies[k].wait_recv()

    @pl.loop(0, tiles)
    def _(n):
        cols = pl.ds(pl.multiple_of(n * TILE, TILE), TILE)
        out_ref[:, cols] = (total[:, cols] + ra[:, cols].astype(F32) + rb[:, cols].astype(F32)).astype(BF16)

    for cp in meta_z:
        cp.wait_send()
    for cp in meta_x:
        cp.wait_send()
    for j in range(4):
        z_done(0, j, v_src(j), vbuf.at[own_rows])
        z_done(1, j, krot.at[j], kbuf.at[own_rows])
        z_done(2, j, qrot.at[j], qbuf.at[q_rows])
    for t in range(2):

        @pl.loop(0, 4)
        def _(i):
            x_out(t, i, 0, xr, l_recv).wait_send()
            x_out(t, i, 1, xl, r_recv).wait_send()
            forward(t, i).wait_send()
            for k, xx in enumerate((x, xl, xr, xo)):
                share(t, k, i, xx).wait_send()

    for step in range(4):

        @pl.loop(0, 4)
        def _(i):
            for e, same, src, dst, to in o_copies(step, order[step], i):

                @pl.when(jnp.logical_not(same))
                def _():
                    remote(src, dst, o_send.at[step, i, e], o_recv.at[step], to).wait_send()

    for cp in y_copies:
        cp.wait_send()


def on_device(q, k, v, w, doc_reset, rand_group, rand_slot, global_blocks):
    numbers = jnp.concatenate([doc_reset, (rand_group * 4 + rand_slot).reshape(-1)])
    meta = jnp.broadcast_to(jnp.pad(numbers, (0, HD - numbers.shape[0]))[None], (8, HD))
    pair = np.arange(HD // 2, dtype=np.float64) * (2.0 / HD)
    freq = np.exp(-pair * math.log(ROPE_BASE)).astype(np.float32)
    freq = jnp.asarray(np.broadcast_to(np.concatenate([freq, freq])[None], (8, HD)).copy())
    vmem = pltpu.VMEM
    dma = pltpu.SemaphoreType.DMA
    any_spec = pl.BlockSpec(memory_space=pl.ANY)
    vmem_spec = pl.BlockSpec(memory_space=pltpu.VMEM)
    return pl.pallas_call(
        kernel,
        out_shape=jax.ShapeDtypeStruct((64, WIDTH), BF16),
        in_specs=[any_spec] * 4 + [vmem_spec] * 2 + [pl.BlockSpec(memory_space=pltpu.SMEM)],
        out_specs=vmem_spec,
        scratch_shapes=[
            vmem((GT, GT), BF16),
            vmem((GT, GT), BF16),
            vmem((4, 4, BLK, HD), BF16),
            vmem((4, 4, BLK, HD), BF16),
            vmem((16, BLK, HD), BF16),
            vmem((128, BLK, HD), BF16),
            vmem((128, BLK, HD), BF16),
            vmem((2 * GT, WIDTH), BF16),
            vmem((NX, NZ, 8, HD), jnp.int32),
            pltpu.SMEM((NZ, 8, HD), jnp.int32),
            vmem((GT, HD), F32),
            vmem((GT, HD), F32),
            vmem((4, 4, BLK, HD), BF16),
            vmem((4 * NZ, 64, HD), BF16),
            vmem((64, WIDTH), BF16),
            vmem((64, WIDTH), BF16),
            vmem((64, WIDTH), BF16),
            vmem((64, WIDTH // 2), BF16),
            vmem((64, WIDTH // 2), BF16),
            vmem((64, WIDTH), BF16),
            vmem((64, WIDTH), BF16),
            vmem((64, WIDTH), F32),
            dma((2,)), dma, dma, dma,
            dma((NZ - 1,)), dma((NZ - 1,)), dma((NX - 1,)), dma((NX - 1,)), dma,
            dma((3, 4)), dma((3, 4)), dma((2, 4, 2)), dma((2, 4)),
            dma((2, 4)), dma((2, 4)), dma((2, 4)), dma((2, 4, 4)), dma((2, 4, 4)),
            dma((4, 4, 2)), dma((4,)), dma((6,)), dma((6,)),
        ],
        compiler_params=pltpu.CompilerParams(
            collective_id=0, has_side_effects=True, vmem_limit_bytes=48 << 20
        ),
        cost_estimate=pl.CostEstimate(flops=3_300_000_000, bytes_accessed=8 << 20, transcendentals=2_200_000),
    )(q, k, v.reshape(4, BLK, GT), w, meta, freq, global_blocks)


def solution(mesh):
    placed = (
        P("ctx", "head"),
        P("ctx", "head"),
        P("ctx", "head"),
        P("head", None),
        P("ctx"),
        P("ctx", None),
        P("ctx", None),
        P(),
    )
    return jax.shard_map(
        on_device, mesh=mesh, in_specs=placed, out_specs=P(("ctx", "head"), None), check_vma=False
    )
```

time: 613 us -> 104 us (0.17)
  the two profiles are of different devices: /device:TPU:1 before, /device:TPU:56 now
where the time goes in v1:
time: 104 us; the launch traced here: 103 us
  Pallas kernels  96.6 us (93%)
  local copies, waits for them, and re-layouts  5.36 us (5%)
  other arithmetic  1.43 us (1%)
    pallas_call x1, Pallas kernels, on_device(): pl.pallas_call(kernel, out_shape=jax.ShapeDtypeStruct((64, WIDTH), BF16),...  96.6 us
    unnamed x11, local copies, waits for them, and re-layouts  5.26 us

profile of v1, /device:TPU:56, one launch (start us, length us, event | category | flops | bytes accessed | tf_op | source)
XLA Modules:
  0.0 103.4 jit_solution(8402375939766953632)
XLA Ops:
  0.0 0.7 multiply_add_fusion
  0.7 0.1 reshape.8
  0.8 0.7 pad_add_fusion
  1.5 0.0 copy-start
  1.5 1.0 %copy-done = bf16[512,512]{1,0:T(8,128)(2,1)S(1)} copy-done((bf16[512,512]{1,0:T(8,128)(2,1)S(1)}, bf16[512,512]{1,0:T(8,128)(2,1)}, u32[]{:S(2)}) %copy-start) | copy-done | bytes 524312
  2.6 0.0 copy-start.1
  2.6 1.0 %copy-done.1 = bf16[512,512]{1,0:T(8,128)(2,1)S(1)} copy-done((bf16[512,512]{1,0:T(8,128)(2,1)S(1)}, bf16[512,512]{1,0:T(8,128)(2,1)}, u32[]{:S(2)}) %copy-start.1) | copy-done | bytes 524312
  3.6 0.0 copy-start.2
  3.6 1.0 %copy-done.2 = bf16[512,512]{1,0:T(8,128)(2,1)S(1)} copy-done((bf16[512,512]{1,0:T(8,128)(2,1)S(1)}, bf16[512,512]{1,0:T(8,128)(2,1)}, u32[]{:S(2)}) %copy-start.2) | copy-done | bytes 524312
  4.7 0.0 copy-start.3
  4.7 0.7 copy-done.3
  5.3 0.0 copy-start.4
  5.3 0.7 copy-done.4
  6.0 96.6 %shard_map.91 = bf16[64,4096]{1,0:T(8,128)(2,1)S(1)} custom-call(bf16[512,512]{1,0:T(8,128)(2,1)S(1)} %copy-done, bf16[512,512]{1,0:T(8,128)(2,1)S(1)} %copy-done.1, bf16[4,128,512]{2,1,0:T(8,128)(2,1)S(1)} %bitcast.1, bf16[512,4096]{1,0:T(8,128)(2,1)} %w_hbm.1, s32[8,128]{1,0:T(8,128)S(1)} %broadcast_in_dim.2.meta_ref, f32[8,128]{1,0:T(8,128)S(1)} %copy-done.4, ...), custom_call_target="tpu_custom_call" | custom-call | flops 3300000000 | bytes 8388608 | tf_op jit(solution)/shard_map/pallas_call | solution.py:460
  102.6 0.8 copy.11
  (2 shorter events, 0.0 us)
Async XLA Ops:
  1.5 1.0 %copy-start = (bf16[512,512]{1,0:T(8,128)(2,1)S(1)}, bf16[512,512]{1,0:T(8,128)(2,1)}, u32[]{:S(2)}) copy-start(bf16[512,512]{1,0:T(8,128)(2,1)} %q_hbm.1) | copy-start | bytes 1572868
  2.6 1.0 %copy-start.1 = (bf16[512,512]{1,0:T(8,128)(2,1)S(1)}, bf16[512,512]{1,0:T(8,128)(2,1)}, u32[]{:S(2)}) copy-start(bf16[512,512]{1,0:T(8,128)(2,1)} %k_hbm.1) | copy-start | bytes 1572868
  3.6 1.0 %copy-start.2 = (bf16[512,512]{1,0:T(8,128)(2,1)S(1)}, bf16[512,512]{1,0:T(8,128)(2,1)}, u32[]{:S(2)}) copy-start(bf16[512,512]{1,0:T(8,128)(2,1)} %param.11) | copy-start | bytes 1572868
  4.7 0.7 copy-start.3
  5.3 0.7 copy-start.4

commit v2 on v1

--- a/solution.py
+++ b/solution.py
@@ -40,9 +40,13 @@
     return sine, cosine
 
 
+def code(*digits):
+    return sum(d * 4**k for k, d in enumerate(digits))
+
+
 def kernel(
-    q_hbm, k_hbm, v_hbm, w_hbm, meta_ref, freq_ref, glob_ref, out_ref,
-    qin, kin, qrot, krot, qbuf, kbuf, vbuf, wbuf, mall, meta_s, cos_t, sin_t,
+    q_hbm, k_hbm, v_hbm, w_hbm, freq_ref, doc_ref, group_ref, slot_ref, glob_ref, out_ref,
+    meta_ref, qin, kin, qrot, krot, qbuf, kbuf, vbuf, wbuf, mall, meta_s, cos_t, sin_t,
     osend, obuf, st1, st2, st3, sa, sb, ra, rb, total,
     in_sem, w_sem, w_send, w_recv,
     mz_send, mz_recv, mx_send, mx_recv, ms_sem,
@@ -79,6 +83,14 @@
     copy_k.start()
     copy_q.start()
 
+    numbers = [doc_ref[b] for b in range(4)]
+    numbers += [group_ref[b, n] * 4 + slot_ref[b, n] for b in range(4) for n in range(3)]
+    spot = lax.broadcasted_iota(jnp.int32, (8, HD), 1)
+    packed = jnp.zeros((8, HD), jnp.int32)
+    for n, number in enumerate(numbers):
+        packed = jnp.where(spot == n, number, packed)
+    meta_ref[...] = packed
+
     barrier = pltpu.get_barrier_semaphore()
     for d in range(NZ):
         for e in range(2):
@@ -105,6 +117,20 @@
     own_rows = rows_of(ctx)
     target_core = z % 2
 
+    place = z % 4
+    near = jnp.where(
+        place == 0, code(0, 1, 2, 3),
+        jnp.where(place == 1, code(1, 0, 2, 3), jnp.where(place == 2, code(2, 3, 1, 0), code(3, 2, 1, 0))),
+    )
+    far = jnp.where(
+        place == 0, code(3, 2, 1, 0),
+        jnp.where(place == 1, code(3, 2, 0, 1), jnp.where(place == 2, code(0, 1, 3, 2), code(0, 1, 2, 3))),
+    )
+    targets = jnp.where(z // 4 == c, near, far)
+    target = [(targets // 4**k) % 4 for k in range(4)]
+    nearest = (z - c + 1) // 2 + 4
+    sender = [(nearest + d) % 4 for d in (0, 3, 1, 2)]
+
     def z_start(t, j, src, dst):
         row = 4 * c + j
         same = (row == z) & (target_core == c)
@@ -129,17 +155,59 @@
     q_rows = pl.ds((z // 2) * 4, 4)
 
     def v_src(j):
-        return v_hbm.at[:, :, j * HD : (j + 1) * HD]
-
-    for j in range(4):
+        return v_hbm.at[:, :, pl.ds(pl.multiple_of(j * HD, HD), HD)]
+
+    bufs = (vbuf, kbuf)
+
+    def group_from(i, xx):
+        return (2 * i + c) * NX + xx
+
+    def x_out(t, i, k, to_x, recv):
+        piece = bufs[t].at[rows_of(group_from(i, x))]
+        return remote(piece, piece, x_send.at[t, i, k], recv.at[t, i], dev(z, to_x, y, c))
+
+    def share(t, k, i, xx):
+        piece = bufs[t].at[rows_of(group_from(i, xx))]
+        return remote(piece, piece, s_send.at[t, k, i], s_recv.at[t, k, i], sib)
+
+    def forward(t, i):
+        from_x = jnp.where(c == 0, xl, xr)
+        to_x = jnp.where(c == 0, xr, xl)
+        piece = bufs[t].at[rows_of(group_from(i, from_x))]
+        return remote(piece, piece, f_send.at[t, i], f_recv.at[t, i], dev(z, to_x, y, c))
+
+    def own_step(t, n):
+        i = sender[n]
+        arrived(bufs[t].at[rows_of(group_from(i, x))], z_recv.at[t, i])
+        x_out(t, i, 0, xr, l_recv).start()
+        x_out(t, i, 1, xl, r_recv).start()
+        share(t, 0, i, x).start()
+
+    def side_step(t, n):
+        i = sender[n]
+        arrived(bufs[t].at[rows_of(group_from(i, xl))], l_recv.at[t, i])
+
+        @pl.when(c == 0)
+        def _():
+            forward(t, i).start()
+
+        arrived(bufs[t].at[rows_of(group_from(i, xr))], r_recv.at[t, i])
+
+        @pl.when(c == 1)
+        def _():
+            forward(t, i).start()
+
+        share(t, 1, i, xl).start()
+        share(t, 2, i, xr).start()
+
+    def far_step(t, n):
+        i = sender[n]
+        arrived(bufs[t].at[rows_of(group_from(i, xo))], f_recv.at[t, i])
+        share(t, 3, i, xo).start()
+
+    for j in target:
         z_start(0, j, v_src(j), vbuf.at[own_rows])
-
-    w_rows = pl.ds(pl.multiple_of(c * GT, GT), GT)
-    w_other = pl.ds(pl.multiple_of((1 - c) * GT, GT), GT)
-    copy_w = remote(w_hbm, wbuf.at[w_rows], w_send, w_recv, sib)
-    copy_w.start()
-    keep_w = local(w_hbm, wbuf.at[w_rows], w_sem)
-    keep_w.start()
+    own_step(0, 0)
 
     for cp in meta_z:
         cp.wait_recv()
@@ -150,6 +218,7 @@
         meta_x.append(cp)
     copy_s = local(mall.at[x], meta_s, ms_sem)
     copy_s.start()
+    own_step(0, 1)
     for cp in meta_x:
         cp.wait_recv()
 
@@ -177,9 +246,8 @@
         sin_t[b * BLK : (b + 1) * BLK, :] = sine * half_sign
 
     def rotate(src, dst, j):
-        @pl.loop(0, 4)
-        def _(b):
-            rows = pl.ds(pl.multiple_of(b * BLK, BLK), BLK)
+        for b in range(4):
+            rows = pl.ds(b * BLK, BLK)
             value = src[rows, j * HD : (j + 1) * HD].astype(F32)
             turned = value * cos_t[rows, :] + pltpu.roll(value, HD // 2, 1) * sin_t[rows, :]
             dst[j, b] = turned.astype(BF16)
@@ -187,69 +255,33 @@
     copy_k.wait()
     for j in range(4):
         rotate(kin, krot, j)
+    for j in target:
         z_start(1, j, krot.at[j], kbuf.at[own_rows])
-
-    bufs = (vbuf, kbuf)
-
-    def group_from(i, xx):
-        return (2 * i + c) * NX + xx
-
-    def x_out(t, i, k, to_x, recv):
-        piece = bufs[t].at[rows_of(group_from(i, x))]
-        return remote(piece, piece, x_send.at[t, i, k], recv.at[t, i], dev(z, to_x, y, c))
-
-    def share(t, k, i, xx):
-        piece = bufs[t].at[rows_of(group_from(i, xx))]
-        return remote(piece, piece, s_send.at[t, k, i], s_recv.at[t, k, i], sib)
-
-    def forward(t, i):
-        from_x = jnp.where(c == 0, xl, xr)
-        to_x = jnp.where(c == 0, xr, xl)
-        piece = bufs[t].at[rows_of(group_from(i, from_x))]
-        return remote(piece, piece, f_send.at[t, i], f_recv.at[t, i], dev(z, to_x, y, c))
-
-    def own_step(t):
-        @pl.loop(0, 4)
-        def _(i):
-            arrived(bufs[t].at[rows_of(group_from(i, x))], z_recv.at[t, i])
-            x_out(t, i, 0, xr, l_recv).start()
-            x_out(t, i, 1, xl, r_recv).start()
-            share(t, 0, i, x).start()
-
-    def side_step(t):
-        @pl.loop(0, 4)
-        def _(i):
-            arrived(bufs[t].at[rows_of(group_from(i, xl))], l_recv.at[t, i])
-
-            @pl.when(c == 0)
-            def _():
-                forward(t, i).start()
-
-            share(t, 1, i, xl).start()
-            arrived(bufs[t].at[rows_of(group_from(i, xr))], r_recv.at[t, i])
-
-            @pl.when(c == 1)
-            def _():
-                forward(t, i).start()
-
-            share(t, 2, i, xr).start()
-
-    def far_step(t):
-        @pl.loop(0, 4)
-        def _(i):
-            arrived(bufs[t].at[rows_of(group_from(i, xo))], f_recv.at[t, i])
-            share(t, 3, i, xo).start()
-
-    own_step(0)
+    own_step(0, 2)
+    own_step(0, 3)
     copy_q.wait()
     for j in range(4):
         rotate(qin, qrot, j)
+
+    own_step(1, 0)
+    for j in target:
         z_start(2, j, qrot.at[j], qbuf.at[q_rows])
-    side_step(0)
-    own_step(1)
-    far_step(0)
-    side_step(1)
-    far_step(1)
+    w_rows = pl.ds(pl.multiple_of(c * GT, GT), GT)
+    w_other = pl.ds(pl.multiple_of((1 - c) * GT, GT), GT)
+    copy_w = remote(w_hbm, wbuf.at[w_rows], w_send, w_recv, sib)
+    copy_w.start()
+    keep_w = local(w_hbm, wbuf.at[w_rows], w_sem)
+    keep_w.start()
+
+    side_step(0, 0)
+    for n in range(1, 4):
+        own_step(1, n)
+        side_step(0, n)
+    for n in range(4):
+        side_step(1, n)
+        far_step(0, n)
+    for n in range(4):
+        far_step(1, n)
 
     def from_sibling(t):
         @pl.loop(0, 4)
@@ -280,7 +312,7 @@
     def attend(step):
         b = order[step]
 
-        @pl.loop(0, 4)
+        @pl.loop(0, 4, unroll=True)
         def _(i):
             zz = 2 * i + c
             block = (zz * NX + x) * 4 + b
@@ -329,7 +361,7 @@
         return b
 
     def project(b, first, last, finish):
-        @pl.loop(first, last)
+        @pl.loop(first, last, unroll=True)
         def _(n):
             cols = pl.ds(pl.multiple_of(n * TILE, TILE), TILE)
             rows = jnp.concatenate([obuf[b * NZ + m] for m in range(NZ)], axis=1)
@@ -364,25 +396,27 @@
         project(b, tiles // 2, tiles, put(st1))
         y_copies[1].start()
 
-    def project_1():
+    def project_1_near():
         b = outputs_of(1)
         project(b, tiles // 2, tiles, put(st2))
-        y_copies[2].start()
-        y_copies[0].wait_recv()
-
+
+    def project_1_far():
         def finish(cols, tile):
             st2[:, cols] = (tile + sa[:, cols].astype(F32)).astype(BF16)
 
-        project(b, 0, tiles // 2, finish)
+        y_copies[0].wait_recv()
+        project(order[1], 0, tiles // 2, finish)
         y_copies[3].start()
 
-    def project_2():
+    def project_2_near():
         b = outputs_of(2)
         project(b, 0, tiles // 2, put(st3))
-        y_copies[4].start()
+
+    def project_2_far():
         y_copies[1].wait_recv()
-
-        @pl.loop(tiles // 2, tiles)
+        b = order[2]
+
+        @pl.loop(tiles // 2, tiles, unroll=True)
         def _(n):
             cols = pl.ds(pl.multiple_of(n * TILE, TILE), TILE)
             near = pl.ds(pl.multiple_of(n * TILE - half, TILE), TILE)
@@ -401,11 +435,17 @@
     keep_w.wait()
     copy_w.wait_send()
     arrived(wbuf.at[w_other], w_recv)
+    attend(2)
     project_0()
-    attend(2)
-    project_1()
+    project_1_near()
     attend(3)
-    project_2()
+    y_copies[0].wait_send()
+    y_copies[2].start()
+    project_2_near()
+    y_copies[1].wait_send()
+    y_copies[4].start()
+    project_1_far()
+    project_2_far()
     project_3()
     for k in (2, 3, 4, 5):
         y_copies[k].wait_recv()
@@ -443,13 +483,11 @@
                 def _():
                     remote(src, dst, o_send.at[step, i, e], o_recv.at[step], to).wait_send()
 
-    for cp in y_copies:
+    for cp in y_copies[2:]:
         cp.wait_send()
 
 
 def on_device(q, k, v, w, doc_reset, rand_group, rand_slot, global_blocks):
-    numbers = jnp.concatenate([doc_reset, (rand_group * 4 + rand_slot).reshape(-1)])
-    meta = jnp.broadcast_to(jnp.pad(numbers, (0, HD - numbers.shape[0]))[None], (8, HD))
     pair = np.arange(HD // 2, dtype=np.float64) * (2.0 / HD)
     freq = np.exp(-pair * math.log(ROPE_BASE)).astype(np.float32)
     freq = jnp.asarray(np.broadcast_to(np.concatenate([freq, freq])[None], (8, HD)).copy())
@@ -460,9 +498,10 @@
     return pl.pallas_call(
         kernel,
         out_shape=jax.ShapeDtypeStruct((64, WIDTH), BF16),
-        in_specs=[any_spec] * 4 + [vmem_spec] * 2 + [pl.BlockSpec(memory_space=pltpu.SMEM)],
+        in_specs=[any_spec] * 4 + [vmem_spec] + [pl.BlockSpec(memory_space=pltpu.SMEM)] * 4,
         out_specs=vmem_spec,
         scratch_shapes=[
+            vmem((8, HD), jnp.int32),
             vmem((GT, GT), BF16),
             vmem((GT, GT), BF16),
             vmem((4, 4, BLK, HD), BF16),
@@ -492,10 +531,10 @@
             dma((4, 4, 2)), dma((4,)), dma((6,)), dma((6,)),
         ],
         compiler_params=pltpu.CompilerParams(
-            collective_id=0, has_side_effects=True, vmem_limit_bytes=48 << 20
+            collective_id=0, has_side_effects=True, vmem_limit_bytes=63 << 20
         ),
         cost_estimate=pl.CostEstimate(flops=3_300_000_000, bytes_accessed=8 << 20, transcendentals=2_200_000),
-    )(q, k, v.reshape(4, BLK, GT), w, meta, freq, global_blocks)
+    )(q, k, v.reshape(4, BLK, GT), w, freq, doc_reset, rand_group, rand_slot, global_blocks)
 
 
 def solution(mesh):

time: 104 us -> 90.7 us (0.87)
  the two profiles are of different devices: /device:TPU:56 before, /device:TPU:1 now
where the time goes in v2:
time: 90.7 us; the launch traced here: 89.3 us
  Pallas kernels  87.4 us (96%)
  local copies, waits for them, and re-layouts  1.87 us (2%)
    pallas_call x1, Pallas kernels, on_device(): pl.pallas_call(kernel, out_shape=jax.ShapeDtypeStruct((64, WIDTH), BF16),...  87.4 us
    unnamed x1, local copies, waits for them, and re-layouts  1.87 us

profile of v2, /device:TPU:1, one launch (start us, length us, event | category | flops | bytes accessed | tf_op | source)
XLA Modules:
  0.0 89.3 jit_solution(1620272960588417194)
XLA Ops:
  0.0 87.4 %shard_map.91 = bf16[64,4096]{1,0:T(8,128)(2,1)} custom-call(bf16[512,512]{1,0:T(8,128)(2,1)} %q_hbm.1, bf16[512,512]{1,0:T(8,128)(2,1)} %k_hbm.1, bf16[4,128,512]{2,1,0:T(8,128)(2,1)} %bitcast.1, bf16[512,4096]{1,0:T(8,128)(2,1)} %w_hbm.1, f32[8,128]{1,0:T(8,128)} %constant.2.clone.freq_ref, s32[4]{0:T(128)} %doc_ref.1, s32[4,3]{1,0:T(4,128)} %group_ref.1, ...), custom_call_target="tpu_custom_call" | custom-call | flops 3300000000 | bytes 8388608 | tf_op jit(solution)/shard_map/pallas_call | solution.py:498
  87.4 1.9 %copy.11 = bf16[64,4096]{1,0:T(8,128)(2,1)} copy(bf16[64,4096]{1,0:T(8,128)(2,1)} %shard_map.91) | data formatting | bytes 1048576

commit v3 on v2

--- a/solution.py
+++ b/solution.py
@@ -14,6 +14,7 @@
 GT = 512
 WIDTH = 4096
 TILE = 512
+CHUNKS = (2, 1, 1)
 ROPE_BASE = 500000.0
 MESH = pl.DeviceIdType.MESH
 F32 = jnp.float32
@@ -111,10 +112,10 @@
         meta_z.append(cp)
     mall[x, z] = meta_ref[...]
 
-    def rows_of(group):
-        return pl.ds(group * 4, 4)
-
-    own_rows = rows_of(ctx)
+    def chunk(base, t, h):
+        size = 4 // CHUNKS[t]
+        return pl.ds(base * 4 + h * size, size)
+
     target_core = z % 2
 
     place = z % 4
@@ -131,10 +132,19 @@
     nearest = (z - c + 1) // 2 + 4
     sender = [(nearest + d) % 4 for d in (0, 3, 1, 2)]
 
-    def z_start(t, j, src, dst):
+    def z_piece(t, h, j):
+        if t == 0:
+            src = v_hbm.at[chunk(0, t, h), :, pl.ds(pl.multiple_of(j * HD, HD), HD)]
+            return src, vbuf.at[chunk(ctx, t, h)]
+        if t == 1:
+            return krot.at[j, chunk(0, t, h)], kbuf.at[chunk(ctx, t, h)]
+        return qrot.at[j, chunk(0, t, h)], qbuf.at[chunk(z // 2, t, h)]
+
+    def z_start(t, h, j):
         row = 4 * c + j
         same = (row == z) & (target_core == c)
-        send, recv = z_send.at[t, j], z_recv.at[t, z // 2]
+        src, dst = z_piece(t, h, j)
+        send, recv = z_send.at[t, h, j], z_recv.at[t, h, z // 2]
 
         @pl.when(same)
         def _():
@@ -144,70 +154,70 @@
         def _():
             remote(src, dst, send, recv, dev(row, x, y, target_core)).start()
 
-    def z_done(t, j, src, dst):
+    def z_done(t, h, j):
         row = 4 * c + j
         same = (row == z) & (target_core == c)
+        src, dst = z_piece(t, h, j)
 
         @pl.when(jnp.logical_not(same))
         def _():
-            remote(src, dst, z_send.at[t, j], z_recv.at[t, z // 2], dev(row, x, y, target_core)).wait_send()
-
-    q_rows = pl.ds((z // 2) * 4, 4)
-
-    def v_src(j):
-        return v_hbm.at[:, :, pl.ds(pl.multiple_of(j * HD, HD), HD)]
+            remote(src, dst, z_send.at[t, h, j], z_recv.at[t, h, z // 2], dev(row, x, y, target_core)).wait_send()
 
     bufs = (vbuf, kbuf)
 
     def group_from(i, xx):
         return (2 * i + c) * NX + xx
 
-    def x_out(t, i, k, to_x, recv):
-        piece = bufs[t].at[rows_of(group_from(i, x))]
-        return remote(piece, piece, x_send.at[t, i, k], recv.at[t, i], dev(z, to_x, y, c))
-
-    def share(t, k, i, xx):
-        piece = bufs[t].at[rows_of(group_from(i, xx))]
-        return remote(piece, piece, s_send.at[t, k, i], s_recv.at[t, k, i], sib)
-
-    def forward(t, i):
+    def x_out(t, h, i, k, to_x, recv):
+        piece = bufs[t].at[chunk(group_from(i, x), t, h)]
+        return remote(piece, piece, x_send.at[t, h, i, k], recv.at[t, h, i], dev(z, to_x, y, c))
+
+    def row_blocks(i, core):
+        return pl.ds((2 * i + core) * 4 * NX, 4 * NX)
+
+    def share(t, i):
+        piece = bufs[t].at[row_blocks(i, c)]
+        return remote(piece, piece, s_send.at[t, i], s_recv.at[t, i], sib)
+
+    def forward(t, h, i):
         from_x = jnp.where(c == 0, xl, xr)
         to_x = jnp.where(c == 0, xr, xl)
-        piece = bufs[t].at[rows_of(group_from(i, from_x))]
-        return remote(piece, piece, f_send.at[t, i], f_recv.at[t, i], dev(z, to_x, y, c))
-
-    def own_step(t, n):
+        piece = bufs[t].at[chunk(group_from(i, from_x), t, h)]
+        return remote(piece, piece, f_send.at[t, h, i], f_recv.at[t, h, i], dev(z, to_x, y, c))
+
+    def own_step(t, h, n):
         i = sender[n]
-        arrived(bufs[t].at[rows_of(group_from(i, x))], z_recv.at[t, i])
-        x_out(t, i, 0, xr, l_recv).start()
-        x_out(t, i, 1, xl, r_recv).start()
-        share(t, 0, i, x).start()
-
-    def side_step(t, n):
+        arrived(bufs[t].at[chunk(group_from(i, x), t, h)], z_recv.at[t, h, i])
+        x_out(t, h, i, 0, xr, l_recv).start()
+        x_out(t, h, i, 1, xl, r_recv).start()
+
+    def side_step(t, h, n):
         i = sender[n]
-        arrived(bufs[t].at[rows_of(group_from(i, xl))], l_recv.at[t, i])
+        arrived(bufs[t].at[chunk(group_from(i, xl), t, h)], l_recv.at[t, h, i])
 
         @pl.when(c == 0)
         def _():
-            forward(t, i).start()
-
-        arrived(bufs[t].at[rows_of(group_from(i, xr))], r_recv.at[t, i])
+            forward(t, h, i).start()
+
+        arrived(bufs[t].at[chunk(group_from(i, xr), t, h)], r_recv.at[t, h, i])
 
         @pl.when(c == 1)
         def _():
-            forward(t, i).start()
-
-        share(t, 1, i, xl).start()
-        share(t, 2, i, xr).start()
-
-    def far_step(t, n):
+            forward(t, h, i).start()
+
+
+    def far_step(t, h, n):
         i = sender[n]
-        arrived(bufs[t].at[rows_of(group_from(i, xo))], f_recv.at[t, i])
-        share(t, 3, i, xo).start()
-
-    for j in target:
-        z_start(0, j, v_src(j), vbuf.at[own_rows])
-    own_step(0, 0)
+        arrived(bufs[t].at[chunk(group_from(i, xo), t, h)], f_recv.at[t, h, i])
+        if h == CHUNKS[t] - 1:
+            share(t, i).start()
+
+    def z_chunk(t, h):
+        if h < CHUNKS[t]:
+            for j in target:
+                z_start(t, h, j)
+
+    z_chunk(0, 0)
 
     for cp in meta_z:
         cp.wait_recv()
@@ -218,7 +228,10 @@
         meta_x.append(cp)
     copy_s = local(mall.at[x], meta_s, ms_sem)
     copy_s.start()
-    own_step(0, 1)
+    for n in range(4):
+        own_step(0, 0, n)
+        if n == 0:
+            z_chunk(0, 1)
     for cp in meta_x:
         cp.wait_recv()
 
@@ -255,17 +268,17 @@
     copy_k.wait()
     for j in range(4):
         rotate(kin, krot, j)
-    for j in target:
-        z_start(1, j, krot.at[j], kbuf.at[own_rows])
-    own_step(0, 2)
-    own_step(0, 3)
-    copy_q.wait()
-    for j in range(4):
-        rotate(qin, qrot, j)
-
-    own_step(1, 0)
-    for j in target:
-        z_start(2, j, qrot.at[j], qbuf.at[q_rows])
+    z_chunk(1, 0)
+    for h in range(1, CHUNKS[0]):
+        for n in range(4):
+            own_step(0, h, n)
+            if n == 0:
+                z_chunk(0, h + 1)
+            side_step(0, h - 1, n)
+        if h == 1:
+            copy_q.wait()
+            for j in range(4):
+                rotate(qin, qrot, j)
     w_rows = pl.ds(pl.multiple_of(c * GT, GT), GT)
     w_other = pl.ds(pl.multiple_of((1 - c) * GT, GT), GT)
     copy_w = remote(w_hbm, wbuf.at[w_rows], w_send, w_recv, sib)
@@ -273,29 +286,38 @@
     keep_w = local(w_hbm, wbuf.at[w_rows], w_sem)
     keep_w.start()
 
-    side_step(0, 0)
-    for n in range(1, 4):
-        own_step(1, n)
-        side_step(0, n)
-    for n in range(4):
-        side_step(1, n)
-        far_step(0, n)
-    for n in range(4):
-        far_step(1, n)
+    last = CHUNKS[0] - 1
+    for h in range(CHUNKS[1]):
+        for n in range(4):
+            own_step(1, h, n)
+            if n == 0:
+                z_chunk(1, h + 1)
+            if h == 0:
+                side_step(0, last, n)
+            else:
+                side_step(1, h - 1, n)
+    z_chunk(2, 0)
+    for h in range(CHUNKS[0]):
+        for n in range(4):
+            if h == 0:
+                side_step(1, CHUNKS[1] - 1, n)
+            far_step(0, h, n)
+    for h in range(CHUNKS[1]):
+        for n in range(4):
+            far_step(1, h, n)
 
     def from_sibling(t):
         @pl.loop(0, 4)
         def _(i):
-            group = (2 * i + 1 - c) * NX
-            for k, xx in enumerate((x, xl, xr, xo)):
-                arrived(bufs[t].at[rows_of(group + xx)], s_recv.at[t, k, i])
+            arrived(bufs[t].at[row_blocks(i, 1 - c)], s_recv.at[t, i])
 
     from_sibling(0)
     from_sibling(1)
 
     @pl.loop(0, 4)
     def _(i):
-        arrived(qbuf.at[pl.ds(i * 4, 4)], z_recv.at[2, i])
+        for h in range(CHUNKS[2]):
+            arrived(qbuf.at[chunk(i, 2, h)], z_recv.at[2, h, i])
 
     copy_s.wait()
 
@@ -430,6 +452,25 @@
         b = outputs_of(3)
         project(b, 0, tiles, put(total))
 
+    def first_phase_left():
+        for cp in meta_z:
+            cp.wait_send()
+        for cp in meta_x:
+            cp.wait_send()
+        for j in range(4):
+            for t in range(3):
+                for h in range(CHUNKS[t]):
+                    z_done(t, h, j)
+        for t in range(2):
+
+            @pl.loop(0, 4)
+            def _(i):
+                for h in range(CHUNKS[t]):
+                    x_out(t, h, i, 0, xr, l_recv).wait_send()
+                    x_out(t, h, i, 1, xl, r_recv).wait_send()
+                    forward(t, h, i).wait_send()
+                share(t, i).wait_send()
+
     attend(0)
     attend(1)
     keep_w.wait()
@@ -439,6 +480,7 @@
     project_0()
     project_1_near()
     attend(3)
+    first_phase_left()
     y_copies[0].wait_send()
     y_copies[2].start()
     project_2_near()
@@ -455,24 +497,6 @@
         cols = pl.ds(pl.multiple_of(n * TILE, TILE), TILE)
         out_ref[:, cols] = (total[:, cols] + ra[:, cols].astype(F32) + rb[:, cols].astype(F32)).astype(BF16)
 
-    for cp in meta_z:
-        cp.wait_send()
-    for cp in meta_x:
-        cp.wait_send()
-    for j in range(4):
-        z_done(0, j, v_src(j), vbuf.at[own_rows])
-        z_done(1, j, krot.at[j], kbuf.at[own_rows])
-        z_done(2, j, qrot.at[j], qbuf.at[q_rows])
-    for t in range(2):
-
-        @pl.loop(0, 4)
-        def _(i):
-            x_out(t, i, 0, xr, l_recv).wait_send()
-            x_out(t, i, 1, xl, r_recv).wait_send()
-            forward(t, i).wait_send()
-            for k, xx in enumerate((x, xl, xr, xo)):
-                share(t, k, i, xx).wait_send()
-
     for step in range(4):
 
         @pl.loop(0, 4)
@@ -491,6 +515,7 @@
     pair = np.arange(HD // 2, dtype=np.float64) * (2.0 / HD)
     freq = np.exp(-pair * math.log(ROPE_BASE)).astype(np.float32)
     freq = jnp.asarray(np.broadcast_to(np.concatenate([freq, freq])[None], (8, HD)).copy())
+    deep = max(CHUNKS)
     vmem = pltpu.VMEM
     dma = pltpu.SemaphoreType.DMA
     any_spec = pl.BlockSpec(memory_space=pl.ANY)
@@ -526,8 +551,8 @@
             vmem((64, WIDTH), F32),
             dma((2,)), dma, dma, dma,
             dma((NZ - 1,)), dma((NZ - 1,)), dma((NX - 1,)), dma((NX - 1,)), dma,
-            dma((3, 4)), dma((3, 4)), dma((2, 4, 2)), dma((2, 4)),
-            dma((2, 4)), dma((2, 4)), dma((2, 4)), dma((2, 4, 4)), dma((2, 4, 4)),
+            dma((3, deep, 4)), dma((3, deep, 4)), dma((2, deep, 4, 2)), dma((2, deep, 4)),
+            dma((2, deep, 4)), dma((2, deep, 4)), dma((2, deep, 4)), dma((2, 4)), dma((2, 4)),
             dma((4, 4, 2)), dma((4,)), dma((6,)), dma((6,)),
         ],
         compiler_params=pltpu.CompilerParams(

time: 90.7 us -> 88 us (0.970); the launches traced: 89.3 us -> 87.8 us
  Pallas kernels: 87.4 us -> 85.9 us
    pallas_call x1, Pallas kernels: 87.4 us -> 85.9 us  [on_device(): pl.pallas_call(kernel, out_shape=jax.ShapeDtypeStruct((64, WIDTH), BF16),...]
where the time goes in v3:
time: 88 us; the launch traced here: 87.8 us
  Pallas kernels  85.9 us (98%)
  local copies, waits for them, and re-layouts  1.87 us (2%)
    pallas_call x1, Pallas kernels, on_device(): pl.pallas_call(kernel, out_shape=jax.ShapeDtypeStruct((64, WIDTH), BF16),...  85.9 us
    unnamed x1, local copies, waits for them, and re-layouts  1.87 us

profile of v3, /device:TPU:1, one launch (start us, length us, event | category | flops | bytes accessed | tf_op | source)
XLA Modules:
  0.0 87.8 jit_solution(11627752284761549681)
XLA Ops:
  0.0 85.9 %shard_map.91 = bf16[64,4096]{1,0:T(8,128)(2,1)} custom-call(bf16[512,512]{1,0:T(8,128)(2,1)} %q_hbm.1, bf16[512,512]{1,0:T(8,128)(2,1)} %k_hbm.1, bf16[4,128,512]{2,1,0:T(8,128)(2,1)} %bitcast.1, bf16[512,4096]{1,0:T(8,128)(2,1)} %w_hbm.1, f32[8,128]{1,0:T(8,128)} %constant.2.clone.freq_ref, s32[4]{0:T(128)} %doc_ref.1, s32[4,3]{1,0:T(4,128)} %group_ref.1, ...), custom_call_target="tpu_custom_call" | custom-call | flops 3300000000 | bytes 8388608 | tf_op jit(solution)/shard_map/pallas_call | solution.py:523
  85.9 1.9 %copy.11 = bf16[64,4096]{1,0:T(8,128)(2,1)} copy(bf16[64,4096]{1,0:T(8,128)(2,1)} %shard_map.91) | data formatting | bytes 1048576

commit v4 on v3

--- a/solution.py
+++ b/solution.py
@@ -489,13 +489,15 @@
     project_1_far()
     project_2_far()
     project_3()
-    for k in (2, 3, 4, 5):
-        y_copies[k].wait_recv()
-
-    @pl.loop(0, tiles)
-    def _(n):
-        cols = pl.ds(pl.multiple_of(n * TILE, TILE), TILE)
-        out_ref[:, cols] = (total[:, cols] + ra[:, cols].astype(F32) + rb[:, cols].astype(F32)).astype(BF16)
+    def add_up(first):
+        for n in range(first, first + tiles // 2):
+            cols = pl.ds(n * TILE, TILE)
+            total[:, cols] = total[:, cols] + (ra if first else rb)[:, cols].astype(F32)
+
+    def finish_half(first):
+        for n in range(first, first + tiles // 2):
+            cols = pl.ds(n * TILE, TILE)
+            out_ref[:, cols] = (total[:, cols] + (rb if first else ra)[:, cols].astype(F32)).astype(BF16)
 
     for step in range(4):
 
@@ -506,6 +508,15 @@
                 @pl.when(jnp.logical_not(same))
                 def _():
                     remote(src, dst, o_send.at[step, i, e], o_recv.at[step], to).wait_send()
+
+    y_copies[2].wait_recv()
+    add_up(tiles // 2)
+    y_copies[4].wait_recv()
+    add_up(0)
+    y_copies[3].wait_recv()
+    finish_half(0)
+    y_copies[5].wait_recv()
+    finish_half(tiles // 2)
 
     for cp in y_copies[2:]:
         cp.wait_send()

time: 88 us -> 87.7 us (level)
  no operation moved by 1% of the time
where the time goes in v4:
time: 87.7 us; the launch traced here: 87.5 us
  Pallas kernels  85.6 us (98%)
  local copies, waits for them, and re-layouts  1.87 us (2%)
    pallas_call x1, Pallas kernels, on_device(): pl.pallas_call(kernel, out_shape=jax.ShapeDtypeStruct((64, WIDTH), BF16),...  85.6 us
    unnamed x1, local copies, waits for them, and re-layouts  1.87 us

profile of v4, /device:TPU:1, one launch (start us, length us, event | category | flops | bytes accessed | tf_op | source)
XLA Modules:
  0.0 87.5 jit_solution(17263273912106087335)
XLA Ops:
  0.0 85.6 %shard_map.91 = bf16[64,4096]{1,0:T(8,128)(2,1)} custom-call(bf16[512,512]{1,0:T(8,128)(2,1)} %q_hbm.1, bf16[512,512]{1,0:T(8,128)(2,1)} %k_hbm.1, bf16[4,128,512]{2,1,0:T(8,128)(2,1)} %bitcast.1, bf16[512,4096]{1,0:T(8,128)(2,1)} %w_hbm.1, f32[8,128]{1,0:T(8,128)} %constant.2.clone.freq_ref, s32[4]{0:T(128)} %doc_ref.1, s32[4,3]{1,0:T(4,128)} %group_ref.1, ...), custom_call_target="tpu_custom_call" | custom-call | flops 3300000000 | bytes 8388608 | tf_op jit(solution)/shard_map/pallas_call | solution.py:534
  85.7 1.9 %copy.11 = bf16[64,4096]{1,0:T(8,128)(2,1)} copy(bf16[64,4096]{1,0:T(8,128)(2,1)} %shard_map.91) | data formatting | bytes 1048576

commit v5 on v4

--- a/solution.py
+++ b/solution.py
@@ -390,6 +390,7 @@
             finish(cols, jnp.dot(rows, wbuf[:, cols], preferred_element_type=F32))
 
     half = WIDTH // 2
+    quarter = WIDTH // 4
     tiles = WIDTH // TILE
     left, right = pl.ds(0, half), pl.ds(half, half)
 
@@ -397,12 +398,14 @@
         return remote(src, dst, y_send.at[k], y_recv.at[k], dev(z, x, yy, c))
 
     y_copies = [
-        y_copy(0, st1.at[:, left], sa, yr),
-        y_copy(1, st1.at[:, right], sb, yl),
+        y_copy(0, st1.at[:, pl.ds(0, quarter)], sa.at[:, pl.ds(0, quarter)], yr),
+        y_copy(1, st1.at[:, pl.ds(half, quarter)], sb.at[:, pl.ds(0, quarter)], yl),
         y_copy(2, st2.at[:, right], ra.at[:, right], yr),
         y_copy(3, st2.at[:, left], ra.at[:, left], yr),
         y_copy(4, st3.at[:, left], rb.at[:, left], yl),
         y_copy(5, st3.at[:, right], rb.at[:, right], yl),
+        y_copy(6, st1.at[:, pl.ds(quarter, quarter)], sa.at[:, pl.ds(quarter, quarter)], yr),
+        y_copy(7, st1.at[:, pl.ds(half + quarter, quarter)], sb.at[:, pl.ds(quarter, quarter)], yl),
     ]
 
     def put(ref):
@@ -413,10 +416,9 @@
 
     def project_0():
         b = outputs_of(0)
-        project(b, 0, tiles // 2, put(st1))
-        y_copies[0].start()
-        project(b, tiles // 2, tiles, put(st1))
-        y_copies[1].start()
+        for part, k in enumerate((0, 6, 1, 7)):
+            project(b, part * tiles // 4, (part + 1) * tiles // 4, put(st1))
+            y_copies[k].start()
 
     def project_1_near():
         b = outputs_of(1)
@@ -427,6 +429,7 @@
             st2[:, cols] = (tile + sa[:, cols].astype(F32)).astype(BF16)
 
         y_copies[0].wait_recv()
+        y_copies[6].wait_recv()
         project(order[1], 0, tiles // 2, finish)
         y_copies[3].start()
 
@@ -436,6 +439,7 @@
 
     def project_2_far():
         y_copies[1].wait_recv()
+        y_copies[7].wait_recv()
         b = order[2]
 
         @pl.loop(tiles // 2, tiles, unroll=True)
@@ -482,9 +486,11 @@
     attend(3)
     first_phase_left()
     y_copies[0].wait_send()
+    y_copies[6].wait_send()
     y_copies[2].start()
     project_2_near()
     y_copies[1].wait_send()
+    y_copies[7].wait_send()
     y_copies[4].start()
     project_1_far()
     project_2_far()
@@ -518,7 +524,7 @@
     y_copies[5].wait_recv()
     finish_half(tiles // 2)
 
-    for cp in y_copies[2:]:
+    for cp in y_copies[2:6]:
         cp.wait_send()
 
 
@@ -564,7 +570,7 @@
             dma((NZ - 1,)), dma((NZ - 1,)), dma((NX - 1,)), dma((NX - 1,)), dma,
             dma((3, deep, 4)), dma((3, deep, 4)), dma((2, deep, 4, 2)), dma((2, deep, 4)),
             dma((2, deep, 4)), dma((2, deep, 4)), dma((2, deep, 4)), dma((2, 4)), dma((2, 4)),
-            dma((4, 4, 2)), dma((4,)), dma((6,)), dma((6,)),
+            dma((4, 4, 2)), dma((4,)), dma((8,)), dma((8,)),
         ],
         compiler_params=pltpu.CompilerParams(
             collective_id=0, has_side_effects=True, vmem_limit_bytes=63 << 20

time: 87.7 us -> 87.3 us (level)
  no operation moved by 1% of the time
where the time goes in v5:
time: 87.3 us; the launch traced here: 87.2 us
  Pallas kernels  85.3 us (98%)
  local copies, waits for them, and re-layouts  1.87 us (2%)
    pallas_call x1, Pallas kernels, on_device(): pl.pallas_call(kernel, out_shape=jax.ShapeDtypeStruct((64, WIDTH), BF16),...  85.3 us
    unnamed x1, local copies, waits for them, and re-layouts  1.87 us

profile of v5, /device:TPU:1, one launch (start us, length us, event | category | flops | bytes accessed | tf_op | source)
XLA Modules:
  0.0 87.2 jit_solution(10430465862041306324)
XLA Ops:
  0.0 85.3 %shard_map.91 = bf16[64,4096]{1,0:T(8,128)(2,1)} custom-call(bf16[512,512]{1,0:T(8,128)(2,1)} %q_hbm.1, bf16[512,512]{1,0:T(8,128)(2,1)} %k_hbm.1, bf16[4,128,512]{2,1,0:T(8,128)(2,1)} %bitcast.1, bf16[512,4096]{1,0:T(8,128)(2,1)} %w_hbm.1, f32[8,128]{1,0:T(8,128)} %constant.2.clone.freq_ref, s32[4]{0:T(128)} %doc_ref.1, s32[4,3]{1,0:T(4,128)} %group_ref.1, ...), custom_call_target="tpu_custom_call" | custom-call | flops 3300000000 | bytes 8388608 | tf_op jit(solution)/shard_map/pallas_call | solution.py:540
  85.3 1.9 %copy.11 = bf16[64,4096]{1,0:T(8,128)(2,1)} copy(bf16[64,4096]{1,0:T(8,128)(2,1)} %shard_map.91) | data formatting | bytes 1048576

commit v6 on v5

--- a/solution.py
+++ b/solution.py
@@ -401,11 +401,12 @@
         y_copy(0, st1.at[:, pl.ds(0, quarter)], sa.at[:, pl.ds(0, quarter)], yr),
         y_copy(1, st1.at[:, pl.ds(half, quarter)], sb.at[:, pl.ds(0, quarter)], yl),
         y_copy(2, st2.at[:, right], ra.at[:, right], yr),
-        y_copy(3, st2.at[:, left], ra.at[:, left], yr),
+        y_copy(3, st2.at[:, pl.ds(0, quarter)], ra.at[:, pl.ds(0, quarter)], yr),
         y_copy(4, st3.at[:, left], rb.at[:, left], yl),
         y_copy(5, st3.at[:, right], rb.at[:, right], yl),
         y_copy(6, st1.at[:, pl.ds(quarter, quarter)], sa.at[:, pl.ds(quarter, quarter)], yr),
         y_copy(7, st1.at[:, pl.ds(half + quarter, quarter)], sb.at[:, pl.ds(quarter, quarter)], yl),
+        y_copy(8, st2.at[:, pl.ds(quarter, quarter)], ra.at[:, pl.ds(quarter, quarter)], yr),
     ]
 
     def put(ref):
@@ -428,10 +429,10 @@
         def finish(cols, tile):
             st2[:, cols] = (tile + sa[:, cols].astype(F32)).astype(BF16)
 
-        y_copies[0].wait_recv()
-        y_copies[6].wait_recv()
-        project(order[1], 0, tiles // 2, finish)
-        y_copies[3].start()
+        for part, came, out in ((0, 0, 3), (1, 6, 8)):
+            y_copies[came].wait_recv()
+            project(order[1], part * tiles // 4, (part + 1) * tiles // 4, finish)
+            y_copies[out].start()
 
     def project_2_near():
         b = outputs_of(2)
@@ -520,11 +521,12 @@
     y_copies[4].wait_recv()
     add_up(0)
     y_copies[3].wait_recv()
+    y_copies[8].wait_recv()
     finish_half(0)
     y_copies[5].wait_recv()
     finish_half(tiles // 2)
 
-    for cp in y_copies[2:6]:
+    for cp in y_copies[2:6] + y_copies[8:]:
         cp.wait_send()
 
 
@@ -570,7 +572,7 @@
             dma((NZ - 1,)), dma((NZ - 1,)), dma((NX - 1,)), dma((NX - 1,)), dma,
             dma((3, deep, 4)), dma((3, deep, 4)), dma((2, deep, 4, 2)), dma((2, deep, 4)),
             dma((2, deep, 4)), dma((2, deep, 4)), dma((2, deep, 4)), dma((2, 4)), dma((2, 4)),
-            dma((4, 4, 2)), dma((4,)), dma((8,)), dma((8,)),
+            dma((4, 4, 2)), dma((4,)), dma((9,)), dma((9,)),
         ],
         compiler_params=pltpu.CompilerParams(
             collective_id=0, has_side_effects=True, vmem_limit_bytes=63 << 20

time: 87.3 us -> 87.4 us (level)
  no operation moved by 1% of the time
where the time goes in v6:
time: 87.4 us; the launch traced here: 87.2 us
  Pallas kernels  85.3 us (98%)
  local copies, waits for them, and re-layouts  1.87 us (2%)
    pallas_call x1, Pallas kernels, on_device(): pl.pallas_call(kernel, out_shape=jax.ShapeDtypeStruct((64, WIDTH), BF16),...  85.3 us
    unnamed x1, local copies, waits for them, and re-layouts  1.87 us

profile of v6, /device:TPU:1, one launch (start us, length us, event | category | flops | bytes accessed | tf_op | source)
XLA Modules:
  0.0 87.2 jit_solution(15851505771109736342)
XLA Ops:
  0.0 85.3 %shard_map.91 = bf16[64,4096]{1,0:T(8,128)(2,1)} custom-call(bf16[512,512]{1,0:T(8,128)(2,1)} %q_hbm.1, bf16[512,512]{1,0:T(8,128)(2,1)} %k_hbm.1, bf16[4,128,512]{2,1,0:T(8,128)(2,1)} %bitcast.1, bf16[512,4096]{1,0:T(8,128)(2,1)} %w_hbm.1, f32[8,128]{1,0:T(8,128)} %constant.2.clone.freq_ref, s32[4]{0:T(128)} %doc_ref.1, s32[4,3]{1,0:T(4,128)} %group_ref.1, ...), custom_call_target="tpu_custom_call" | custom-call | flops 3300000000 | bytes 8388608 | tf_op jit(solution)/shard_map/pallas_call | solution.py:542
  85.3 1.9 %copy.11 = bf16[64,4096]{1,0:T(8,128)(2,1)} copy(bf16[64,4096]{1,0:T(8,128)(2,1)} %shard_map.91) | data formatting | bytes 1048576
